TPU v7x, 32 devices: a whole 2x2x4 slice. The times are simulated.
32 devices in a mesh: grp: 4 (over y, x), seq: 4 (over z), mlp: 2 (over core).
Axes of the slice: x: 2, y: 2, z: 4, core: 2. Of those that a mesh axis runs over, the one named last changes fastest.
Arguments:
- queries: bfloat16 [16, 4, 4096], P('grp'), may hold values from -6 to 6
- new_keys: bfloat16 [16, 4, 4096], P(('grp', 'seq')), may hold values from -6 to 6
- new_values: bfloat16 [16, 4, 4096], P(('grp', 'seq')), may hold values from -6 to 6
- prefix_keys: bfloat16 [4, 2048, 4096], P('grp', ('seq', 'mlp')), may hold values from -250 to 250
- prefix_values: bfloat16 [4, 2048, 4096], P('grp', ('seq', 'mlp')), may hold values from -6 to 6
- tail_keys: bfloat16 [16, 256, 4096], P(('grp', 'seq'), 'mlp'), may hold values from -6 to 6
- tail_values: bfloat16 [16, 256, 4096], P(('grp', 'seq'), 'mlp'), may hold values from -6 to 6
- prefix_len: int32 [4], P('grp'), may hold values from 1 to 2048, as said below
- tail_len: int32 [16], P('grp'), may hold values from 0 to 256, as said below
- resid: bfloat16 [16, 4, 4096], P('grp', None, ('seq', 'mlp')), may hold values from -12 to 12
- w_out: bfloat16 [4096, 4096], P(None, ('seq', 'mlp')), may hold values from -0.09375 to 0.09375
- ln_gain: bfloat16 [4096], P(('seq', 'mlp')), may hold values from 0.25 to 1.75
- w_up: bfloat16 [4096, 16384], P(('seq', 'mlp'), 'grp'), may hold values from -0.09375 to 0.09375
- w_down: bfloat16 [16384, 4096], P('grp', ('seq', 'mlp')), may hold values from -0.046875 to 0.046875
Outputs:
- out: float32 [16, 4, 4096], P('grp', None, ('seq', 'mlp'))
Inputs may be any that keep to these rules, and one draw needn't show every extreme that they name: `prefix_len`: every group's live prefix is 1 to 2048 slots; in every draw some group's prefix fills all 2048 slots. `tail_len`: A request's live tail is 0 to 256 slots; in every draw some request's tail fills all 256 slots.
All inputs are finite; a program needn't handle non-finite values.
Results may differ from a plain program's by a relative error of at most 0.0075.
Values may be sent and summed in bfloat16 or wider, within the bound.
A program may use at most 128 MiB of HBM per device.

v0:
```python
import math
import jax
import jax.numpy as jnp
from jax import lax
from jax.sharding import PartitionSpec as P

D = 4096
H = 32
NEG = -1e30


def merged(value, axis, join):
    pieces = jax.tree.map(lambda part: lax.all_gather(part, axis), value)
    head = jax.tree.map(lambda part: part[0], pieces)
    tail = jax.tree.map(lambda part: part[1:], pieces)
    so_far, _ = lax.scan(lambda so_far, piece: (join(so_far, piece), None), head, tail)
    return so_far


def head_slopes(count):
    return jnp.power(2.0, -8.0 * (jnp.arange(count, dtype=jnp.float32) + 1.0) / count)


def attend(query_rows, key_block, value_block, query_pos, key_pos, key_mask):
    head_count = query_rows.shape[1]
    inv_scale = 1.0 / math.sqrt(query_rows.shape[2])
    scores = (
        jnp.einsum("qhd,khd->hqk", query_rows, key_block, preferred_element_type=jnp.float32)
        * inv_scale
    )
    distance = (query_pos[:, None] - key_pos[None, :]).astype(jnp.float32)
    scores = scores - head_slopes(head_count)[:, None, None] * distance[None, :, :]
    scores = jnp.where(key_mask, scores, NEG)
    row_max = jnp.max(scores, axis=2)
    weights = jnp.where(key_mask, jnp.exp(scores - row_max[:, :, None]), 0.0)
    weight_sum = jnp.sum(weights, axis=2)
    mixed_sum = jnp.einsum(
        "hqk,khd->qhd",
        weights.astype(jnp.bfloat16),
        value_block,
        preferred_element_type=jnp.float32,
    )
    return (row_max.T, weight_sum.T, mixed_sum)


def join_parts(first, second):
    best_max = jnp.maximum(first[0], second[0])
    factor_one = jnp.exp(first[0] - best_max)
    factor_two = jnp.exp(second[0] - best_max)
    return (
        best_max,
        first[1] * factor_one + second[1] * factor_two,
        first[2] * factor_one[:, :, None] + second[2] * factor_two[:, :, None],
    )


def body(
    queries,
    new_keys,
    new_values,
    prefix_keys,
    prefix_values,
    tail_keys,
    tail_values,
    prefix_len,
    tail_len,
    resid,
    w_out,
    ln_gain,
    w_up,
    w_down,
):
    group_req, step_count, model_width = queries.shape
    head_dim = model_width // H
    row_count = group_req * step_count
    seq_index = lax.axis_index("seq")
    core_index = lax.axis_index("mlp")
    block_len = prefix_keys.shape[1]
    tail_block = tail_keys.shape[1]
    block_start = (seq_index * lax.axis_size("mlp") + core_index) * block_len
    prefix_end = prefix_len[0]
    step_index = jnp.arange(step_count, dtype=jnp.int32)
    query_pos = prefix_end + jnp.repeat(tail_len, step_count) + jnp.tile(step_index, group_req)
    query_rows = queries.reshape(row_count, H, head_dim)
    key_pos = block_start + jnp.arange(block_len, dtype=jnp.int32)
    key_live = key_pos < prefix_end
    own_len = lax.dynamic_index_in_dim(tail_len, seq_index, 0, keepdims=False)
    own_rows = lax.dynamic_slice_in_dim(query_rows, seq_index * step_count, step_count, 0)
    own_pos = prefix_end + own_len + step_index
    tail_index = core_index * tail_block + jnp.arange(tail_block, dtype=jnp.int32)
    partial_value = attend(
        query_rows,
        prefix_keys[0].reshape(block_len, H, head_dim),
        prefix_values[0].reshape(block_len, H, head_dim),
        query_pos,
        key_pos,
        key_live[None, None, :],
    )
    tail_result = attend(
        own_rows,
        tail_keys[0].reshape(tail_block, H, head_dim),
        tail_values[0].reshape(tail_block, H, head_dim),
        own_pos,
        prefix_end + tail_index,
        (tail_index < own_len)[None, None, :],
    )
    self_mask = (step_index[None, :] <= step_index[:, None]) & (core_index == 0)
    self_result = attend(
        own_rows,
        new_keys[0].reshape(step_count, H, head_dim),
        new_values[0].reshape(step_count, H, head_dim),
        own_pos,
        own_pos,
        self_mask[None, :, :],
    )
    own_slice = tuple(
        (
            lax.dynamic_slice_in_dim(member, seq_index * step_count, step_count, 0)
            for member in partial_value
        )
    )
    own_part = join_parts(join_parts(own_slice, tail_result), self_result)
    partial_value = tuple(
        (
            lax.dynamic_update_slice_in_dim(member, update, seq_index * step_count, 0)
            for member, update in zip(partial_value, own_part)
        )
    )
    row_max, weight_sum, mixed_sum = merged(
        (partial_value[0], partial_value[1], partial_value[2]), ("seq", "mlp"), join_parts
    )
    attention = (
        (mixed_sum / weight_sum[:, :, None]).astype(jnp.bfloat16).reshape(row_count, model_width)
    )
    width_block = resid.shape[2]
    stream = resid.astype(jnp.float32).reshape(row_count, width_block) + jnp.dot(
        attention, w_out, preferred_element_type=jnp.float32
    )
    row_sums, squares = lax.psum(
        (jnp.sum(stream, axis=1), jnp.sum(stream * stream, axis=1)), ("seq", "mlp")
    )
    row_mean = row_sums / D
    row_var = squares / D - row_mean * row_mean
    hidden = (
        (stream - row_mean[:, None])
        * lax.rsqrt(row_var[:, None] + 1e-05)
        * ln_gain.astype(jnp.float32)
    ).astype(jnp.bfloat16)
    lifted = jnp.dot(
        lax.all_gather(hidden, "grp", axis=0, tiled=True), w_up, preferred_element_type=jnp.float32
    )
    summed = lax.psum(lifted, ("seq", "mlp"))
    activated = jax.nn.gelu(summed, approximate=False).astype(jnp.bfloat16)
    projected = lax.psum_scatter(
        jnp.dot(activated, w_down, preferred_element_type=jnp.float32),
        "grp",
        scatter_dimension=0,
        tiled=True,
    )
    return (stream + projected).reshape(group_req, step_count, width_block)


def solution(mesh):
    return jax.shard_map(
        body,
        mesh=mesh,
        in_specs=(
            P("grp", None, None),
            P(("grp", "seq"), None, None),
            P(("grp", "seq"), None, None),
            P("grp", ("seq", "mlp"), None),
            P("grp", ("seq", "mlp"), None),
            P(("grp", "seq"), "mlp", None),
            P(("grp", "seq"), "mlp", None),
            P("grp"),
            P("grp"),
            P("grp", None, ("seq", "mlp")),
            P(None, ("seq", "mlp")),
            P(("seq", "mlp")),
            P(("seq", "mlp"), "grp"),
            P("grp", ("seq", "mlp")),
        ),
        out_specs=P("grp", None, ("seq", "mlp")),
        check_vma=False,
    )
```

profile of v0, /device:TPU:0, one launch (start us, length us, event | category | flops | bytes accessed | tf_op | source)
XLA Modules:
  0.0 181.5 jit_solution(5606925134826433128)
XLA Ops:
  7.4 1.2 dynamic_slice.28
  9.2 0.6 fusion.102
  9.8 0.1 subtract_convert_fusion.1
  9.8 0.1 subtract_convert_fusion.2
  9.9 1.1 reshape.182
  11.0 1.4 copy.98
  12.5 0.7 fusion.143
  13.2 0.1 copy.70
  13.3 0.2 fusion.78
  13.5 0.1 copy.78
  13.6 0.1 iota_add_fusion
  13.7 0.1 add.152
  13.8 0.5 copy.97
  14.3 0.1 subtract_convert_fusion
  14.4 1.2 fusion.142
  15.6 0.3 fusion.70
  15.8 0.1 constant_dynamic-slice_fusion
  15.9 0.1 copy.95
  16.0 0.1 copy.96
  16.1 0.2 fusion.81
  16.3 0.1 copy.72
  16.4 0.1 fusion.135
  16.5 0.1 fusion.88
  16.6 0.1 copy.85
  16.7 0.1 copy.87
  16.8 0.1 copy.88
  16.9 0.5 copy.99
  17.4 1.0 fusion.3
  18.4 0.2 copy-done.3
  18.6 0.2 copy.100
  18.9 0.1 copy.91
  18.9 0.1 copy.89
  19.1 0.5 fusion.22
  19.6 0.2 fusion.19
  19.8 0.8 copy.92
  20.7 0.1 copy.82
  20.8 0.2 dynamic_update_slice.13
  21.0 15.8 %all_gather.32 = f32[8,16,32]{2,1,0:T(8,128)S(1)} all-gather(f32[1,16,32]{2,1,0:T(8,128)S(1)} %copy.83), channel_id=1, replica_groups=mesh['grp'=4,'seq'=4,'mlp'=2] {'seq','mlp'}, dimensions={0}, use_global_device_ids=true | all-gather | bytes 18432 | tf_op jit(solution)/shard_map/all_gather | solution.py:13
  36.9 0.1 copy.75
  37.0 0.2 dynamic_update_slice.12
  37.2 0.1 copy.76
  37.2 14.1 %all_gather.29 = f32[8,16,32]{2,1,0:T(8,128)S(1)} all-gather(f32[1,16,32]{2,1,0:T(8,128)S(1)} %copy.76), channel_id=1, replica_groups=mesh['grp'=4,'seq'=4,'mlp'=2] {'seq','mlp'}, dimensions={0}, use_global_device_ids=true | all-gather | bytes 18432 | tf_op jit(solution)/shard_map/all_gather | solution.py:13
  51.4 1.7 all-gather.2.cloned.1.call-done
  53.1 1.7 slice.29
  54.8 1.0 slice_bitcast_fusion
  55.8 2.2 %while.14 = (s32[]{:T(128)}, f32[16,32]{1,0:T(8,128)S(1)}, f32[16,32]{1,0:T(8,128)S(1)}, f32[16,32,128]{2,1,0:T(8,128)S(1)}, f32[7,16,32]{2,1,0:T(8,128)S(1)}, /...) while((s32[]{:T(128)}, f32[16,32]{1,0:T(8,128)S(1)}, f32[16,32]{1,0:T(8,128)S(1)}, ...), condition=%wide.region_7.8_spmd, body=%wide.region_6.7_spmd.sunk | while | flops 199682 | bytes 807005 | solution.py:16
  55.8 0.3 fusion.153
  56.1 0.3 fusion.153
  56.4 0.3 fusion.153
  56.8 0.3 fusion.153
  57.1 0.3 fusion.153
  57.4 0.3 fusion.153
  57.7 0.3 fusion.153
  58.0 0.1 divide_convert_fusion
  58.1 3.0 %fusion.137 = (f32[16]{0:T(128)S(1)}, f32[16]{0:T(128)S(1)}, f32[16,512]{1,0:T(8,128)S(1)}) fusion(f32[16,512]{1,0:T(8,128)S(1)} %reshape.186, bf16[4096,512]{1,0:T(8,128)(2,1)} %param.26, bf16[2,8,32,128]{3,2,1,0:T(8,128)(2,1)S(1)} %bitcast.177), kind=kOutput, calls=%fused_computation.181 | convolution fusion | flops 67141600 | bytes 4391040 | tf_op jit(solution)/shard_map/dot_general | solution.py:136
  61.1 15.5 %all-reduce = (f32[16]{0:T(128)S(1)}, f32[16]{0:T(128)S(1)}) all-reduce(f32[16]{0:T(128)S(1)} %get-tuple-element.60, f32[16]{0:T(128)S(1)} %get-tuple-element.59), channel_id=1, replica_groups=mesh['grp'=4,'seq'=4,'mlp'=2] {'seq','mlp'}, use_global_device_ids=true, to_apply=%region_11.12 | all-reduce | flops 32 | bytes 256 | tf_op jit(solution)/shard_map/psum | solution.py:139
  76.5 0.1 multiply_convert_fusion
  76.6 8.1 %all_gather.36 = bf16[64,512]{1,0:T(8,128)(2,1)S(1)} all-gather(bf16[16,512]{1,0:T(8,128)(2,1)S(1)} %multiply_convert_fusion), channel_id=1, replica_groups=mesh['grp'=4,'seq'=4,'mlp'=2] {'grp'}, dimensions={0}, use_global_device_ids=true | all-gather | bytes 81920 | tf_op jit(solution)/shard_map/all_gather | solution.py:150
  84.8 4.1 %fusion.144 = f32[64,4096]{1,0:T(8,128)} fusion(bf16[64,512]{1,0:T(8,128)(2,1)S(1)} %all_gather.36, bf16[512,4096]{1,0:T(8,128)(2,1)} %param.28), kind=kOutput, calls=%fused_computation.184 | convolution fusion | flops 268435456 | bytes 5308416 | tf_op jit(solution)/shard_map/dot_general | solution.py:149
  88.9 56.1 %all-reduce.3.cloned.1.call-done = f32[64,4096]{1,0:T(8,128)} async-done(((f32[64,4096]{1,0:T(8,128)}), f32[64,4096]{1,0:T(8,128)}) %all-reduce.3.cloned.1.call-update) | async-done | bytes 1048592 | tf_op jit(solution)/shard_map/psum | solution.py:152
  145.1 5.5 %fusion.37 = f32[64,512]{1,0:T(8,128)} fusion(bf16[4096,512]{1,0:T(8,128)(2,1)} %param.29, f32[64,4096]{1,0:T(8,128)} %all-reduce.3.cloned.1.call-done), kind=kOutput, calls=%fused_computation.49 | convolution fusion | flops 285474816 | bytes 5373952 | tf_op jit(solution)/shard_map/dot_general | solution.py:155
  150.6 22.9 %reduce-scatter.2.cloned.1.call-done = f32[16,512]{1,0:T(8,128)} async-done(((f32[64,512]{1,0:T(8,128)}), f32[16,512]{1,0:T(8,128)}) %reduce-scatter.2.cloned.1.call-update) | async-done | bytes 32784 | tf_op jit(solution)/shard_map/reduce_scatter | solution.py:154
  173.6 0.8 add.168
  174.3 0.6 reshape.184
  (45 shorter events, 0.5 us)
Async XLA Ops:
  6.5 13.1 %copy-start = (bf16[1,4,4096]{2,1,0:T(4,128)(2,1)S(1)}, bf16[1,4,4096]{2,1,0:T(4,128)(2,1)}, u32[]{:S(2)}) copy-start(bf16[1,4,4096]{2,1,0:T(4,128)(2,1)} %param.18) | copy-start | bytes 98308
  6.5 7.1 %copy-start.7 = (s32[4]{0:T(128)S(1)}, s32[4]{0:T(128)}, u32[]{:S(2)}) copy-start(s32[4]{0:T(128)} %param.24) | copy-start | bytes 52
  6.5 7.2 %copy-start.1 = (bf16[1,256,4096]{2,1,0:T(8,128)(2,1)S(1)}, bf16[1,256,4096]{2,1,0:T(8,128)(2,1)}, u32[]{:S(2)}) copy-start(bf16[1,256,4096]{2,1,0:T(8,128)(2,1)} %param.19) | copy-start | bytes 6291460
  6.5 46.6 %all-gather.2.cloned.1.call-start = ((), (), s32[]{:S(2)}) async-start(), calls=%async_computation.1 | async-start | bytes 2359296 | tf_op jit(solution)/shard_map/all_gather | solution.py:13
  14.3 1.8 copy-start.4
  14.3 2.6 %copy-start.2 = (bf16[1,256,4096]{2,1,0:T(8,128)(2,1)S(1)}, bf16[1,256,4096]{2,1,0:T(8,128)(2,1)}, u32[]{:S(2)}) copy-start(bf16[1,256,4096]{2,1,0:T(8,128)(2,1)} %param.20) | copy-start | bytes 6291460
  17.3 1.2 copy-start.3
  18.8 32.5 %copy-start.5 = (bf16[4,4,512]{2,1,0:T(4,128)(2,1)S(1)}, bf16[4,4,512]{2,1,0:T(4,128)(2,1)}, u32[]{:S(2)}) copy-start(bf16[4,4,512]{2,1,0:T(4,128)(2,1)} %param.25) | copy-start | bytes 49156
  18.8 32.5 %copy-start.6 = (bf16[512]{0:T(512)(128)(2,1)S(1)}, bf16[512]{0:T(512)(128)(2,1)}, u32[]{:S(2)}) copy-start(bf16[512]{0:T(512)(128)(2,1)} %param.27) | copy-start | bytes 3076
  20.6 124.4 %all-reduce.3.cloned.1.call-start = ((), (), s32[]{:S(2)}) async-start(), calls=%async_computation.2 | async-start | bytes 2097152 | tf_op jit(solution)/shard_map/psum | solution.py:152
  88.9 84.7 %reduce-scatter.2.cloned.1.call-start = ((), (), s32[]{:S(2)}) async-start(), calls=%async_computation.3 | async-start | bytes 163840 | tf_op jit(solution)/shard_map/reduce_scatter | solution.py:154
Sparse Core Ops, SparseCore 0:
  20.8 32.3 all-gather.1
  89.0 56.0 all-reduce.2
  150.7 22.7 reduce-scatter.1
where the time goes:
time: 182 us; the launch traced here: 181 us
  waiting for transfers between devices  80.9 us (44%)
  blocking collectives  53.5 us (29%)
  matrix products  16.5 us (9%)
  between operations  14.8 us (8%)
  local copies, waits for them, and re-layouts  11 us (6%)
  other arithmetic  4.55 us (2%)
    psum x1, waiting for transfers between devices, body(): summed = lax.psum(lifted, ('seq', 'mlp'))  56.1 us
    all_gather x2, blocking collectives, merged(): pieces = jax.tree.map(lambda part: lax.all_gather(part, axis), value)  29.9 us
    reduce_scatter x1, waiting for transfers between devices, body(): lax.psum_scatter(jnp.dot(activated, w_down, preferred_element_type=jnp.fl...  22.9 us
    psum x1, blocking collectives, body(): lax.psum((jnp.sum(stream, axis=1), jnp.sum(stream * stream, axis=1)), ('s...  15.5 us
    all_gather x1, blocking collectives, body(): lax.all_gather(hidden, 'grp', axis=0, tiled=True)  8.13 us
    dot_general x1, matrix products, body(): jnp.dot(activated, w_down, preferred_element_type=jnp.float32)  5.52 us
    dot_general x1, matrix products, body(): jnp.dot(lax.all_gather(hidden, 'grp', axis=0, tiled=True), w_up, preferre...  4.1 us
  transfers between devices with their start and end apart: 3, of which 3 were waited for; matrix products, arithmetic and copies ran while one was open for 0% of the time, Pallas kernels for 0%

commit v1 on v0

--- a/solution.py
+++ b/solution.py
@@ -149,7 +149,15 @@
     lifted = jnp.dot(
         lax.all_gather(hidden, "grp", axis=0, tiled=True), w_up, preferred_element_type=jnp.float32
     )
-    summed = lax.psum(lifted, ("seq", "mlp"))
+
+    def _meet_patches(z):
+        bus_axis = "seq"
+        axis_tag = "mlp"
+        for dd in (axis_tag, bus_axis):
+            z = lax.psum(z, axis_name=dd)
+        return z
+
+    summed = _meet_patches(lifted)
     activated = jax.nn.gelu(summed, approximate=False).astype(jnp.bfloat16)
     projected = lax.psum_scatter(
         jnp.dot(activated, w_down, preferred_element_type=jnp.float32),

time: 182 us -> 199 us (1.093)
  waiting for transfers between devices: 80.9 us -> 97.6 us
    psum x1 -> x2, waiting for transfers between devices: 56.1 us -> 72.4 us  [_meet_patches(): z = lax.psum(z, axis_name=dd)]
  transfers between devices with their start and end apart: 3 -> 4, of which waited for: 3 -> 4; matrix products, arithmetic and copies ran while one was open for 0% -> 0% of each run, Pallas kernels for 0% -> 0%
where the time goes in v1:
time: 199 us; the launch traced here: 198 us
  waiting for transfers between devices  97.6 us (49%)
  blocking collectives  53.5 us (27%)
  matrix products  16.5 us (8%)
  between operations  14.8 us (7%)
  local copies, waits for them, and re-layouts  11 us (6%)
  other arithmetic  4.55 us (2%)
    psum x2, waiting for transfers between devices, _meet_patches(): z = lax.psum(z, axis_name=dd)  72.4 us
    all_gather x2, blocking collectives, merged(): pieces = jax.tree.map(lambda part: lax.all_gather(part, axis), value)  29.9 us
    reduce_scatter x1, waiting for transfers between devices, body(): lax.psum_scatter(jnp.dot(activated, w_down, preferred_element_type=jnp.fl...  23.4 us
    psum x1, blocking collectives, body(): lax.psum((jnp.sum(stream, axis=1), jnp.sum(stream * stream, axis=1)), ('s...  15.5 us
    all_gather x1, blocking collectives, body(): lax.all_gather(hidden, 'grp', axis=0, tiled=True)  8.13 us
    dot_general x1, matrix products, body(): jnp.dot(activated, w_down, preferred_element_type=jnp.float32)  5.51 us
    dot_general x1, matrix products, body(): jnp.dot(lax.all_gather(hidden, 'grp', axis=0, tiled=True), w_up, preferre...  4.1 us
  transfers between devices with their start and end apart: 4, of which 4 were waited for; matrix products, arithmetic and copies ran while one was open for 0% of the time, Pallas kernels for 0%

profile of v1, /device:TPU:0, one launch (start us, length us, event | category | flops | bytes accessed | tf_op | source)
XLA Modules:
  0.0 198.3 jit_solution(11466417132712250505)
XLA Ops:
  7.4 1.2 dynamic_slice.28
  9.2 0.6 fusion.102
  9.8 0.1 subtract_convert_fusion.1
  9.8 0.1 subtract_convert_fusion.2
  9.9 1.1 reshape.182
  11.0 1.4 copy.98
  12.5 0.7 fusion.143
  13.2 0.1 copy.70
  13.3 0.2 fusion.78
  13.5 0.1 copy.78
  13.6 0.1 iota_add_fusion
  13.7 0.1 add.154
  13.8 0.5 copy.97
  14.3 0.1 subtract_convert_fusion
  14.4 1.2 fusion.142
  15.6 0.3 fusion.70
  15.8 0.1 constant_dynamic-slice_fusion
  15.9 0.1 copy.95
  16.0 0.1 copy.96
  16.1 0.2 fusion.81
  16.3 0.1 copy.72
  16.4 0.1 fusion.135
  16.5 0.1 fusion.88
  16.6 0.1 copy.85
  16.7 0.1 copy.87
  16.8 0.1 copy.88
  16.9 0.5 copy.99
  17.4 1.0 fusion.3
  18.4 0.2 copy-done.3
  18.6 0.2 copy.100
  18.9 0.1 copy.91
  18.9 0.1 copy.89
  19.1 0.5 fusion.22
  19.6 0.2 fusion.19
  19.8 0.8 copy.92
  20.7 0.1 copy.82
  20.8 0.2 dynamic_update_slice.13
  21.0 15.8 %all_gather.32 = f32[8,16,32]{2,1,0:T(8,128)S(1)} all-gather(f32[1,16,32]{2,1,0:T(8,128)S(1)} %copy.83), channel_id=1, replica_groups=mesh['grp'=4,'seq'=4,'mlp'=2] {'seq','mlp'}, dimensions={0}, use_global_device_ids=true | all-gather | bytes 18432 | tf_op jit(solution)/shard_map/all_gather | solution.py:13
  36.9 0.1 copy.75
  37.0 0.2 dynamic_update_slice.12
  37.2 14.1 %all_gather.29 = f32[8,16,32]{2,1,0:T(8,128)S(1)} all-gather(f32[1,16,32]{2,1,0:T(8,128)S(1)} %copy.76), channel_id=1, replica_groups=mesh['grp'=4,'seq'=4,'mlp'=2] {'seq','mlp'}, dimensions={0}, use_global_device_ids=true | all-gather | bytes 18432 | tf_op jit(solution)/shard_map/all_gather | solution.py:13
  51.4 1.7 all-gather.2.cloned.1.call-done
  53.1 1.7 slice.29
  54.8 1.0 slice_bitcast_fusion
  55.8 2.2 %while.14 = (s32[]{:T(128)}, f32[16,32]{1,0:T(8,128)S(1)}, f32[16,32]{1,0:T(8,128)S(1)}, f32[16,32,128]{2,1,0:T(8,128)S(1)}, f32[7,16,32]{2,1,0:T(8,128)S(1)}, /...) while((s32[]{:T(128)}, f32[16,32]{1,0:T(8,128)S(1)}, f32[16,32]{1,0:T(8,128)S(1)}, ...), condition=%wide.region_7.8_spmd, body=%wide.region_6.7_spmd.sunk | while | flops 199682 | bytes 807005 | solution.py:16
  55.8 0.3 fusion.153
  56.1 0.3 fusion.153
  56.4 0.3 fusion.153
  56.8 0.3 fusion.153
  57.1 0.3 fusion.153
  57.4 0.3 fusion.153
  57.7 0.3 fusion.153
  58.0 0.1 divide_convert_fusion
  58.1 3.0 %fusion.137 = (f32[16]{0:T(128)S(1)}, f32[16]{0:T(128)S(1)}, f32[16,512]{1,0:T(8,128)S(1)}) fusion(f32[16,512]{1,0:T(8,128)S(1)} %reshape.186, bf16[4096,512]{1,0:T(8,128)(2,1)} %param.26, bf16[2,8,32,128]{3,2,1,0:T(8,128)(2,1)S(1)} %bitcast.177), kind=kOutput, calls=%fused_computation.181 | convolution fusion | flops 67141600 | bytes 4391040 | tf_op jit(solution)/shard_map/dot_general | solution.py:136
  61.1 15.5 %all-reduce = (f32[16]{0:T(128)S(1)}, f32[16]{0:T(128)S(1)}) all-reduce(f32[16]{0:T(128)S(1)} %get-tuple-element.60, f32[16]{0:T(128)S(1)} %get-tuple-element.59), channel_id=1, replica_groups=mesh['grp'=4,'seq'=4,'mlp'=2] {'seq','mlp'}, use_global_device_ids=true, to_apply=%region_11.12 | all-reduce | flops 32 | bytes 256 | tf_op jit(solution)/shard_map/psum | solution.py:139
  76.5 0.1 multiply_convert_fusion
  76.6 8.1 %all_gather.36 = bf16[64,512]{1,0:T(8,128)(2,1)S(1)} all-gather(bf16[16,512]{1,0:T(8,128)(2,1)S(1)} %multiply_convert_fusion), channel_id=1, replica_groups=mesh['grp'=4,'seq'=4,'mlp'=2] {'grp'}, dimensions={0}, use_global_device_ids=true | all-gather | bytes 81920 | tf_op jit(solution)/shard_map/all_gather | solution.py:150
  84.8 4.1 %fusion.144 = f32[64,4096]{1,0:T(8,128)} fusion(bf16[64,512]{1,0:T(8,128)(2,1)S(1)} %all_gather.36, bf16[512,4096]{1,0:T(8,128)(2,1)} %param.28), kind=kOutput, calls=%fused_computation.184 | convolution fusion | flops 268435456 | bytes 5308416 | tf_op jit(solution)/shard_map/dot_general | solution.py:149
  88.9 16.9 %all-reduce.4.cloned.1.call-done = f32[64,4096]{1,0:T(8,128)} async-done(((f32[64,4096]{1,0:T(8,128)}), f32[64,4096]{1,0:T(8,128)}) %all-reduce.4.cloned.1.call-update) | async-done | bytes 1048592 | tf_op jit(solution)/shard_map/psum | solution.py:157
  105.9 55.5 %all-reduce.6.cloned.1.call-done = f32[64,4096]{1,0:T(8,128)} async-done(((f32[64,4096]{1,0:T(8,128)}), f32[64,4096]{1,0:T(8,128)}) %all-reduce.6.cloned.1.call-update) | async-done | bytes 1048592 | tf_op jit(solution)/shard_map/psum | solution.py:157
  161.4 5.5 %fusion.37 = f32[64,512]{1,0:T(8,128)} fusion(bf16[4096,512]{1,0:T(8,128)(2,1)} %param.29, f32[64,4096]{1,0:T(8,128)} %all-reduce.6.cloned.1.call-done), kind=kOutput, calls=%fused_computation.49 | convolution fusion | flops 285474816 | bytes 5373952 | tf_op jit(solution)/shard_map/dot_general | solution.py:163
  166.9 23.4 %reduce-scatter.2.cloned.1.call-done = f32[16,512]{1,0:T(8,128)} async-done(((f32[64,512]{1,0:T(8,128)}), f32[16,512]{1,0:T(8,128)}) %reduce-scatter.2.cloned.1.call-update) | async-done | bytes 32784 | tf_op jit(solution)/shard_map/reduce_scatter | solution.py:162
  190.3 0.8 add.170
  191.1 0.6 reshape.184
  (48 shorter events, 0.7 us)
Async XLA Ops:
  6.5 13.1 %copy-start = (bf16[1,4,4096]{2,1,0:T(4,128)(2,1)S(1)}, bf16[1,4,4096]{2,1,0:T(4,128)(2,1)}, u32[]{:S(2)}) copy-start(bf16[1,4,4096]{2,1,0:T(4,128)(2,1)} %param.18) | copy-start | bytes 98308
  6.5 7.1 %copy-start.7 = (s32[4]{0:T(128)S(1)}, s32[4]{0:T(128)}, u32[]{:S(2)}) copy-start(s32[4]{0:T(128)} %param.24) | copy-start | bytes 52
  6.5 7.2 %copy-start.1 = (bf16[1,256,4096]{2,1,0:T(8,128)(2,1)S(1)}, bf16[1,256,4096]{2,1,0:T(8,128)(2,1)}, u32[]{:S(2)}) copy-start(bf16[1,256,4096]{2,1,0:T(8,128)(2,1)} %param.19) | copy-start | bytes 6291460
  6.5 46.6 %all-gather.2.cloned.1.call-start = ((), (), s32[]{:S(2)}) async-start(), calls=%async_computation.1 | async-start | bytes 2359296 | tf_op jit(solution)/shard_map/all_gather | solution.py:13
  14.3 1.8 copy-start.4
  14.3 2.6 %copy-start.2 = (bf16[1,256,4096]{2,1,0:T(8,128)(2,1)S(1)}, bf16[1,256,4096]{2,1,0:T(8,128)(2,1)}, u32[]{:S(2)}) copy-start(bf16[1,256,4096]{2,1,0:T(8,128)(2,1)} %param.20) | copy-start | bytes 6291460
  17.3 1.2 copy-start.3
  18.8 32.5 %copy-start.5 = (bf16[4,4,512]{2,1,0:T(4,128)(2,1)S(1)}, bf16[4,4,512]{2,1,0:T(4,128)(2,1)}, u32[]{:S(2)}) copy-start(bf16[4,4,512]{2,1,0:T(4,128)(2,1)} %param.25) | copy-start | bytes 49156
  18.8 32.5 %copy-start.6 = (bf16[512]{0:T(512)(128)(2,1)S(1)}, bf16[512]{0:T(512)(128)(2,1)}, u32[]{:S(2)}) copy-start(bf16[512]{0:T(512)(128)(2,1)} %param.27) | copy-start | bytes 3076
  20.6 85.2 %all-reduce.4.cloned.1.call-start = ((), (), s32[]{:S(2)}) async-start(), calls=%async_computation.2 | async-start | bytes 2097152 | tf_op jit(solution)/shard_map/psum | solution.py:157
  88.9 72.5 %all-reduce.6.cloned.1.call-start = ((), (), s32[]{:S(2)}) async-start(), calls=%async_computation.3 | async-start | bytes 2097152 | tf_op jit(solution)/shard_map/psum | solution.py:157
  105.9 84.4 %reduce-scatter.2.cloned.1.call-start = ((), (), s32[]{:S(2)}) async-start(), calls=%async_computation.4 | async-start | bytes 163840 | tf_op jit(solution)/shard_map/reduce_scatter | solution.py:162
Sparse Core Ops, SparseCore 0:
  20.8 32.3 all-gather.1
  89.0 16.8 all-reduce.3
  108.4 52.9 all-reduce.5
  167.1 23.2 reduce-scatter.1
